TPU v7x, 256 devices: a whole 4x4x8 slice. The times are simulated.
256 devices in a mesh: grp: 8 (over y, core), mem: 32 (over x, z).
Axes of the slice: x: 4, y: 4, z: 8, core: 2. Of those that a mesh axis runs over, the one named last changes fastest.
Arguments:
- old_rows: bfloat16 [65536, 1024], P(('grp', 'mem')), may hold values from -24 to 24
- new_rows: bfloat16 [65536, 1024], P(('grp', 'mem')), may hold values from -6 to 6
- list_ids: int32 [65536], P(('grp', 'mem')), may hold values from 0 to 65535, as said below
- owner_map: int32 [65536], replicated, may hold values from 0 to 31, as said below
Outputs:
- owner_rows: float32 [131072, 1024], P(('grp', 'mem'))
- rotation: bfloat16 [1024, 1024], P('mem')
Inputs may be any that keep to these rules, and one draw needn't show every extreme that they name: `list_ids`: in each device's block of 256 rows, at most 16 rows belong to lists of any one owner; in every group some owner receives exactly 16 rows from every device of the group. `owner_map`: every owner holds 65536 // 32 lists.
All inputs are finite; a program needn't handle non-finite values.
Results may differ from a plain program's by a relative error of at most 0.023.
Values may be sent and summed in bfloat16 or wider, within the bound.
No kernel may reach another device: no remote copies, remote signals or barrier semaphores. Data moves between devices by JAX's collectives and lax.ppermute only.
A program may use at most 64 MiB of HBM per device.

v0:
```python
import math
import jax
import jax.numpy as jnp
from jax import lax
from jax.sharding import PartitionSpec as P

ITERS = 2
EPSILON = 1e-06
COEFF_ONE = 3.4445
COEFF_THREE = -4.775
COEFF_FIVE = 2.0315


def combine_terms(iterate, first, second):
    return (
        COEFF_ONE * iterate.astype(jnp.float32)
        + COEFF_THREE * first.astype(jnp.float32)
        + COEFF_FIVE * second
    ).astype(jnp.bfloat16)


def local(old_rows, new_rows, list_ids, owner_map):
    features = old_rows.shape[1]
    row_total = old_rows.shape[0]
    members = lax.axis_size("mem")
    block_rows = features // members
    scaling = 0.25 * math.sqrt(features)
    partial_value = jnp.dot(old_rows.T, new_rows, preferred_element_type=jnp.float32)
    covariance = lax.psum(partial_value, ("grp", "mem"))
    squares = jnp.sum(covariance * covariance)
    iterate = (covariance * scaling / jnp.sqrt(squares + EPSILON)).astype(jnp.bfloat16)
    for sweep in range(ITERS):
        gram = jnp.dot(iterate, iterate.T, preferred_element_type=jnp.float32).astype(jnp.bfloat16)
        first = jnp.dot(gram, iterate, preferred_element_type=jnp.float32).astype(jnp.bfloat16)
        second = jnp.dot(gram, first, preferred_element_type=jnp.float32)
        iterate = combine_terms(iterate, first, second)
    own_rows = lax.dynamic_slice_in_dim(iterate, lax.axis_index("mem") * block_rows, block_rows, 0)
    capacity = 2 * row_total // members
    owner_of_row = owner_map[list_ids]
    onehot = (owner_of_row[:, None] == jnp.arange(members, dtype=jnp.int32)[None, :]).astype(
        jnp.int32
    )
    earlier = jnp.cumsum(onehot, axis=0) - onehot
    slot_index = owner_of_row * capacity + jnp.sum(earlier * onehot, axis=1)
    payload = jnp.dot(old_rows, iterate, preferred_element_type=jnp.float32)
    buffer = jnp.zeros((members * capacity, features), jnp.float32).at[slot_index].set(payload)
    buffer = buffer.reshape(members, capacity, features)
    arrived = lax.all_to_all(buffer, "mem", split_axis=0, concat_axis=0, tiled=True).reshape(
        members * capacity, features
    )
    return (arrived, own_rows)


def solution(mesh):
    in_specs = (P(("grp", "mem"), None), P(("grp", "mem"), None), P(("grp", "mem")), P())
    out_specs = (P(("grp", "mem"), None), P("mem", None))
    return jax.shard_map(local, mesh=mesh, in_specs=in_specs, out_specs=out_specs, check_vma=False)
```

profile of v0, /device:TPU:64, one launch (start us, length us, event | category | flops | bytes accessed | tf_op | source)
XLA Modules:
  0.0 378.5 jit_solution(7004765975214528384)
XLA Ops:
  7.2 1.0 copy-done
  8.2 3.8 fusion.8
  12.0 0.7 copy-done.3
  12.7 0.3 copy-done.2
  12.9 1.7 gather_fusion
  14.7 0.6 reduce-window.6
  15.3 0.2 slice_reduce_fusion
  15.6 265.5 %all-reduce.2.cloned.1.call-done = f32[1024,1024]{1,0:T(8,128)} async-done(((f32[1024,1024]{1,0:T(8,128)}), f32[1024,1024]{1,0:T(8,128)}) %all-reduce.2.cloned.1.call-update) | async-done | bytes 4194320 | tf_op jit(solution)/shard_map/psum | solution.py:29
  281.1 3.9 %multiply_reduce_fusion = f32[]{:T(128)} fusion(f32[1024,1024]{1,0:T(8,128)} %all-reduce.2.cloned.1.call-done), kind=kLoop, calls=%fused_computation.5 | loop fusion | flops 2097151 | bytes 4194308 | tf_op jit(solution)/shard_map/reduce_sum | solution.py:30
  285.7 2.8 divide_convert_fusion
  288.5 2.4 convolution_convert_fusion.1
  290.9 2.3 fusion.9
  293.2 2.6 add_convert_fusion.1
  295.8 2.4 convolution_convert_fusion
  298.2 2.3 fusion.10
  300.5 2.8 add_convert_fusion
  303.3 1.3 copy-done.1
  304.7 0.8 convolution_bitcast_fusion
  305.5 0.3 copy.8
  305.8 2.8 scatter_custom_fusion
  308.6 11.8 %all-to-all-start = ((f32[32,16,1024]{2,1,0:T(8,128)}), f32[32,16,1024]{2,1,0:T(8,128)S(1)}, u32[]{:S(2)}, u32[]{:S(2)}) async-start(f32[32,16,1024]{2,1,0:T(8,128)} %bitcast.43), calls=%async_computation | async-start | bytes 4194304 | tf_op jit(solution)/shard_map/all_to_all | solution.py:48
  320.4 1.5 constant_dynamic-slice_fusion
  321.9 48.5 %all-to-all-done = f32[32,16,1024]{2,1,0:T(8,128)S(1)} async-done(((f32[32,16,1024]{2,1,0:T(8,128)}), f32[32,16,1024]{2,1,0:T(8,128)S(1)}, u32[]{:S(2)}, u32[]{:S(2)}) %all-to-all-start) | async-done | bytes 2097184 | tf_op jit(solution)/shard_map/all_to_all | solution.py:48
  370.4 1.3 copy.13
  (14 shorter events, 0.2 us)
Async XLA Ops:
  7.2 1.0 copy-start
  7.2 273.9 %all-reduce.2.cloned.1.call-start = ((), (), s32[]{:S(2)}) async-start(), calls=%async_computation.1 | async-start | bytes 8388608 | tf_op jit(solution)/shard_map/psum | solution.py:29
  12.0 0.7 copy-start.3
  12.0 1.0 copy-start.2
  303.3 1.4 copy-start.1
  308.6 61.7 %all-to-all-start = ((f32[32,16,1024]{2,1,0:T(8,128)}), f32[32,16,1024]{2,1,0:T(8,128)S(1)}, u32[]{:S(2)}, u32[]{:S(2)}) async-start(f32[32,16,1024]{2,1,0:T(8,128)} %bitcast.43), calls=%async_computation | async-start | bytes 4194304 | tf_op jit(solution)/shard_map/all_to_all | solution.py:48
Sparse Core Ops, SparseCore 0:
  13.5 267.5 all-reduce.1
where the time goes:
time: 379 us
  waiting for transfers between devices  314 us (83%)
  matrix products  19.3 us (5%)
  between operations  14.9 us (4%)
  starting transfers between devices  11.8 us (3%)
  local copies, waits for them, and re-layouts  11.1 us (3%)
  other arithmetic  7.41 us (2%)
    psum x1, waiting for transfers between devices, local(): covariance = lax.psum(partial_value, ('grp', 'mem'))  265 us
    all_to_all x1, waiting for transfers between devices, local(): lax.all_to_all(buffer, 'mem', split_axis=0, concat_axis=0, tiled=True)  48.5 us
    all_to_all x1, starting transfers between devices, local(): lax.all_to_all(buffer, 'mem', split_axis=0, concat_axis=0, tiled=True)  11.8 us
  transfers between devices with their start and end apart: 2, of which 2 were waited for; matrix products, arithmetic and copies ran while one was open for 1% of the time, Pallas kernels for 0%

commit v1 on v0

--- a/solution.py
+++ b/solution.py
@@ -26,7 +26,7 @@
     block_rows = features // members
     scaling = 0.25 * math.sqrt(features)
     partial_value = jnp.dot(old_rows.T, new_rows, preferred_element_type=jnp.float32)
-    covariance = lax.psum(partial_value, ("grp", "mem"))
+    covariance = lax.psum(lax.psum(partial_value, "mem"), "grp")
     squares = jnp.sum(covariance * covariance)
     iterate = (covariance * scaling / jnp.sqrt(squares + EPSILON)).astype(jnp.bfloat16)
     for sweep in range(ITERS):

time: 379 us -> 351 us (0.926)
  waiting for transfers between devices: 314 us -> 286 us
    psum x1 -> x2, waiting for transfers between devices: 265 us -> 240 us  [local(): covariance = lax.psum(lax.psum(partial_value, 'mem'), 'grp')]
  transfers between devices with their start and end apart: 2 -> 3, of which waited for: 2 -> 3; matrix products, arithmetic and copies ran while one was open for 1% -> 1% of each run, Pallas kernels for 0% -> 0%
where the time goes in v1:
time: 351 us; the launch traced here: 349 us
  waiting for transfers between devices  286 us (81%)
  matrix products  19.4 us (6%)
  between operations  14.9 us (4%)
  local copies, waits for them, and re-layouts  11.1 us (3%)
  starting transfers between devices  10 us (3%)
  other arithmetic  7.41 us (2%)
    psum x2, waiting for transfers between devices, local(): covariance = lax.psum(lax.psum(partial_value, 'mem'), 'grp')  240 us
    all_to_all x1, waiting for transfers between devices, local(): lax.all_to_all(buffer, 'mem', split_axis=0, concat_axis=0, tiled=True)  45.9 us
    all_to_all x1, starting transfers between devices, local(): lax.all_to_all(buffer, 'mem', split_axis=0, concat_axis=0, tiled=True)  9.97 us
  transfers between devices with their start and end apart: 3, of which 3 were waited for; matrix products, arithmetic and copies ran while one was open for 1% of the time, Pallas kernels for 0%

profile of v1, /device:TPU:64, one launch (start us, length us, event | category | flops | bytes accessed | tf_op | source)
XLA Modules:
  0.0 348.9 jit_solution(9694412791120650395)
XLA Ops:
  7.2 1.0 copy-done
  8.2 3.8 %fusion.8 = f32[1024,1024]{1,0:T(8,128)} fusion(bf16[256,1024]{1,0:T(8,128)(2,1)S(1)} %copy-done, bf16[256,1024]{1,0:T(8,128)(2,1)} %param.5), kind=kOutput, calls=%fused_computation.27 | convolution fusion | flops 536870912 | bytes 5242880 | tf_op jit(solution)/shard_map/dot_general | solution.py:28
  12.0 165.9 %all-reduce.3.cloned.1.call-done = f32[1024,1024]{1,0:T(8,128)} async-done(((f32[1024,1024]{1,0:T(8,128)}), f32[1024,1024]{1,0:T(8,128)}) %all-reduce.3.cloned.1.call-update) | async-done | bytes 4194320 | tf_op jit(solution)/shard_map/psum | solution.py:29
  178.0 0.7 copy-done.3
  178.7 0.3 copy-done.2
  179.0 1.7 gather_fusion
  180.7 0.6 reduce-window.6
  181.6 74.2 %all-reduce.5.cloned.1.call-done = f32[1024,1024]{1,0:T(8,128)} async-done(((f32[1024,1024]{1,0:T(8,128)}), f32[1024,1024]{1,0:T(8,128)}) %all-reduce.5.cloned.1.call-update) | async-done | bytes 4194320 | tf_op jit(solution)/shard_map/psum | solution.py:29
  255.9 3.9 %multiply_reduce_fusion = f32[]{:T(128)} fusion(f32[1024,1024]{1,0:T(8,128)} %all-reduce.5.cloned.1.call-done), kind=kLoop, calls=%fused_computation.5 | loop fusion | flops 2097151 | bytes 4194308 | tf_op jit(solution)/shard_map/reduce_sum | solution.py:30
  260.4 2.8 divide_convert_fusion
  263.2 2.4 convolution_convert_fusion.1
  265.6 2.3 fusion.9
  267.9 2.6 add_convert_fusion.1
  270.6 2.4 convolution_convert_fusion
  272.9 2.3 fusion.10
  275.3 2.8 add_convert_fusion
  278.1 1.3 copy-done.1
  279.5 0.8 convolution_bitcast_fusion
  280.2 0.3 copy.8
  280.6 2.8 scatter_custom_fusion
  283.4 10.0 %all-to-all-start = ((f32[32,16,1024]{2,1,0:T(8,128)}), f32[32,16,1024]{2,1,0:T(8,128)S(1)}, u32[]{:S(2)}, u32[]{:S(2)}) async-start(f32[32,16,1024]{2,1,0:T(8,128)} %bitcast.43), calls=%async_computation | async-start | bytes 4194304 | tf_op jit(solution)/shard_map/all_to_all | solution.py:48
  293.4 1.5 constant_dynamic-slice_fusion
  294.9 45.9 %all-to-all-done = f32[32,16,1024]{2,1,0:T(8,128)S(1)} async-done(((f32[32,16,1024]{2,1,0:T(8,128)}), f32[32,16,1024]{2,1,0:T(8,128)S(1)}, u32[]{:S(2)}, u32[]{:S(2)}) %all-to-all-start) | async-done | bytes 2097184 | tf_op jit(solution)/shard_map/all_to_all | solution.py:48
  340.7 1.3 copy.14
  (17 shorter events, 0.5 us)
Async XLA Ops:
  7.2 1.0 copy-start
  7.2 170.8 %all-reduce.3.cloned.1.call-start = ((), (), s32[]{:S(2)}) async-start(), calls=%async_computation.1 | async-start | bytes 8388608 | tf_op jit(solution)/shard_map/psum | solution.py:29
  12.0 243.9 %all-reduce.5.cloned.1.call-start = ((), (), s32[]{:S(2)}) async-start(), calls=%async_computation.2 | async-start | bytes 8388608 | tf_op jit(solution)/shard_map/psum | solution.py:29
  178.0 0.7 copy-start.3
  178.0 1.0 copy-start.2
  278.1 1.4 copy-start.1
  283.4 57.3 %all-to-all-start = ((f32[32,16,1024]{2,1,0:T(8,128)}), f32[32,16,1024]{2,1,0:T(8,128)S(1)}, u32[]{:S(2)}, u32[]{:S(2)}) async-start(f32[32,16,1024]{2,1,0:T(8,128)} %bitcast.43), calls=%async_computation | async-start | bytes 4194304 | tf_op jit(solution)/shard_map/all_to_all | solution.py:48
Sparse Core Ops, SparseCore 0:
  12.1 165.8 all-reduce.2
  180.5 75.3 all-reduce.4
